TPU v7x, 256 devices: a whole 4x4x8 slice. The times are simulated.
256 devices in a mesh: dp: 32 (over z_hi, x, core), tensor: 8 (over z_lo, y).
Axes of the slice: x: 4, y: 4, z: 8 (z_hi: 4, z_lo: 2; z = z_hi * 2 + z_lo), core: 2. Of those that a mesh axis runs over, the one named last changes fastest.
Arguments:
- gate_pre: bfloat16 [16384, 13312], P('dp', 'tensor'), may hold values from -6 to 6
- up_pre: bfloat16 [16384, 13312], P('dp', 'tensor'), may hold values from -6 to 6
- out_grad: bfloat16 [16384, 5120], P('dp', 'tensor'), may hold values from -0.046875 to 0.046875
- master: float32 [5120, 13312], P('dp', 'tensor'), may hold values from -6 to 6
- moment_one: float32 [5120, 13312], P('dp', 'tensor'), may hold values from -3 to 3
- moment_two: float32 [5120, 13312], P('dp', 'tensor'), may hold values from 0.05 to 1
Outputs:
- master_new: float32 [5120, 13312], P('dp', 'tensor')
- moment_one_new: float32 [5120, 13312], P('dp', 'tensor')
- moment_two_new: float32 [5120, 13312], P('dp', 'tensor')
- serving: bfloat16 [5120, 13312], P(('dp', 'tensor'))
All inputs are finite; a program needn't handle non-finite values.
Results may differ from a plain program's by a relative error of at most 0.006.
Values may be sent and summed in bfloat16 or wider, within the bound.
No kernel may reach another device: no remote copies, remote signals or barrier semaphores. Data moves between devices by JAX's collectives and lax.ppermute only.
A program may use at most 128 MiB of HBM per device.

v0:
```python
import jax
import jax.numpy as jnp
from jax import lax
from jax.sharding import PartitionSpec as P


def on_device(gate_pre, up_pre, out_grad, master, moment_one, moment_two):
    hidden = (jax.nn.silu(gate_pre.astype(jnp.float32)) * up_pre.astype(jnp.float32)).astype(
        jnp.bfloat16
    )
    contract = (((0,), (0,)), ((), ()))
    full_grad = lax.all_gather(out_grad, "tensor", axis=1, tiled=True)
    grad = lax.psum_scatter(
        lax.dot_general(full_grad, hidden, contract, preferred_element_type=jnp.float32).astype(
            jnp.bfloat16
        ),
        "dp",
        scatter_dimension=0,
        tiled=True,
    ).astype(jnp.float32)
    moment_one_new = 0.9 * moment_one + 0.1 * grad
    moment_two_new = 0.95 * moment_two + 0.05 * grad * grad
    first = moment_one_new / (1.0 - 0.9**20)
    second = moment_two_new / (1.0 - 0.95**20)
    master_new = master - 0.01 * (first / (jnp.sqrt(second) + 1e-08) + 0.1 * master)
    serving = lax.all_to_all(
        master_new.astype(jnp.bfloat16), "tensor", split_axis=0, concat_axis=1, tiled=True
    )
    return (master_new, moment_one_new, moment_two_new, serving)


def solution(mesh):
    placed = (
        P("dp", "tensor"),
        P("dp", "tensor"),
        P("dp", "tensor"),
        P("dp", "tensor"),
        P("dp", "tensor"),
        P("dp", "tensor"),
    )
    return jax.shard_map(
        on_device,
        mesh=mesh,
        in_specs=placed,
        out_specs=(
            P("dp", "tensor"),
            P("dp", "tensor"),
            P("dp", "tensor"),
            P(("dp", "tensor"), None),
        ),
        check_vma=False,
    )
```

profile of v0, /device:TPU:4, one launch (start us, length us, event | category | flops | bytes accessed | tf_op | source)
XLA Modules:
  0.0 310.6 jit_solution(16241422006121291722)
XLA Ops:
  7.2 0.0 all-gather.2.cloned.1.call-start
  7.2 0.7 all-gather.2.cloned.1.call-update
  7.9 0.0 reduce-scatter.4.cloned.1.call-start
  7.9 69.9 %all-gather.2.cloned.1.call-done = bf16[512,5120]{1,0:T(8,128)(2,1)} async-done(((bf16[512,640]{1,0:T(8,128)(2,1)}), bf16[512,5120]{1,0:T(8,128)(2,1)}) %all-gather.2.cloned.1.call-update) | async-done | bytes 5242896 | tf_op jit(solution)/shard_map/all_gather | solution.py:12
  77.8 15.9 %fusion = bf16[5120,1664]{0,1:T(8,128)(2,1)} fusion(bf16[512,5120]{1,0:T(8,128)(2,1)} %all-gather.2.cloned.1.call-done, bf16[512,1664]{1,0:T(8,128)(2,1)} %param.7, bf16[512,1664]{1,0:T(8,128)(2,1)} %param.6), kind=kOutput, calls=%fused_computation.1 | convolution fusion | flops 8739487744 | bytes 25690112 | tf_op jit(solution)/shard_map/dot_general | solution.py:14
  93.8 22.5 %copy.46 = bf16[5120,1664]{1,0:T(8,128)(2,1)} copy(bf16[5120,1664]{0,1:T(8,128)(2,1)} %fusion) | data formatting | bytes 34078720
  116.2 0.0 copy-start
  116.2 0.0 copy-start.1
  116.2 0.0 reduce-scatter.4.cloned.1.call-update
  116.3 167.6 %reduce-scatter.4.cloned.1.call-done = bf16[160,1664]{1,0:T(8,128)(2,1)} async-done(((bf16[5120,1664]{1,0:T(8,128)(2,1)}), bf16[160,1664]{1,0:T(8,128)(2,1)}) %reduce-scatter.4.cloned.1.call-update) | async-done | bytes 532496 | tf_op jit(solution)/shard_map/reduce_scatter | solution.py:13
  283.9 0.0 copy-done
  283.9 0.0 copy-done.1
  283.9 3.6 %fusion.11 = (bf16[160,1664]{1,0:T(8,128)(2,1)S(1)}, f32[160,1664]{1,0:T(8,128)}, f32[160,1664]{1,0:T(8,128)}, f32[160,1664]{1,0:T(8,128)}) fusion(f32[160,1664]{1,0:T(8,128)S(1)} %copy-done, bf16[160,1664]{1,0:T(8,128)(2,1)} %reduce-scatter.4.cloned.1.call-done, f32[160,1664]{1,0:T(8,128)S(1)} %copy-done.1, f32[160,1664]{1,0:T(8,128)} %param.11), kind=kLoop, calls=%fused_computation.16 | loop fusion | flops 4526080 | bytes 7454720 | tf_op jit(solution)/shard_map/convert_element_type | solution.py:27
  287.5 0.1 all_to_all.14
  287.6 15.2 %all_to_all.19 = bf16[8,20,1664]{2,1,0:T(8,128)(2,1)S(1)} all-to-all(bf16[8,20,1664]{2,1,0:T(8,128)(2,1)S(1)} %all_to_all.14), channel_id=1, replica_groups=mesh['dp'=32,'tensor'=8] {'tensor'}, dimensions={0} | all-to-all | bytes 1064960 | tf_op jit(solution)/shard_map/all_to_all | solution.py:26
  302.8 0.1 copy.45
  302.9 0.9 copy.48
  (1 shorter events, 0.0 us)
Async XLA Ops:
  7.2 70.7 %all-gather.2.cloned.1.call-start = ((), (), s32[]{:S(2)}) async-start(), calls=%async_computation.2 | async-start | bytes 5898240 | tf_op jit(solution)/shard_map/all_gather | solution.py:12
  7.9 276.0 %reduce-scatter.4.cloned.1.call-start = ((), (), s32[]{:S(2)}) async-start(), calls=%async_computation.3 | async-start | bytes 17571840 | tf_op jit(solution)/shard_map/reduce_scatter | solution.py:13
  116.2 167.6 %copy-start = (f32[160,1664]{1,0:T(8,128)S(1)}, f32[160,1664]{1,0:T(8,128)}, u32[]{:S(2)}) copy-start(f32[160,1664]{1,0:T(8,128)} %param.9) | copy-start | bytes 3194884
  116.2 167.6 %copy-start.1 = (f32[160,1664]{1,0:T(8,128)S(1)}, f32[160,1664]{1,0:T(8,128)}, u32[]{:S(2)}) copy-start(f32[160,1664]{1,0:T(8,128)} %param.10) | copy-start | bytes 3194884
Sparse Core Ops, SparseCore 0:
  9.8 67.9 all-gather.1
  116.4 167.4 reduce-scatter.3
where the time goes:
time: 311 us
  waiting for transfers between devices  238 us (77%)
  local copies, waits for them, and re-layouts  23.6 us (8%)
  matrix products  15.9 us (5%)
  blocking collectives  15.2 us (5%)
  between operations  14.1 us (5%)
  other arithmetic  3.61 us (1%)
    reduce_scatter x1, waiting for transfers between devices, on_device(): lax.psum_scatter(lax.dot_general(full_grad, hidden, contract, preferred_e...  168 us
    all_gather x1, waiting for transfers between devices, on_device(): full_grad = lax.all_gather(out_grad, 'tensor', axis=1, tiled=True)  69.9 us
    unnamed x7, local copies, waits for them, and re-layouts  23.4 us
    dot_general x1, matrix products, on_device(): lax.dot_general(full_grad, hidden, contract, preferred_element_type=jnp.f...  15.9 us
    all_to_all x1, blocking collectives, on_device(): lax.all_to_all(master_new.astype(jnp.bfloat16), 'tensor', split_axis=0, c...  15.2 us
  transfers between devices with their start and end apart: 2, of which 2 were waited for; matrix products, arithmetic and copies ran while one was open for 0% of the time, Pallas kernels for 0%

commit v1 on v0

v1 whole, which is shorter than its diff:
```python
import jax
import jax.numpy as jnp
import numpy as np
from jax import lax
from jax.experimental import pallas as pl
from jax.experimental.pallas import tpu as pltpu
from jax.sharding import Mesh, PartitionSpec as P

BF = jnp.bfloat16
F32 = jnp.float32
SIZES = {"zh": 4, "x": 4, "c": 2, "zl": 2, "y": 4}
CHUNKS = ((0, 896), (896, 768))


def shift(value, axis, by):
    n = SIZES[axis]
    return lax.ppermute(value, axis, [(i, (i + by) % n) for i in range(n)])


def matmul_kernel(slab_ref, *refs):
    units, tails, pieces = refs[0:7], refs[7:9], refs[9:14]
    out_ref, a_all = refs[14], refs[15]

    @pl.when(pl.program_id(0) == 0)
    def _():
        for u in range(8):
            slab = slab_ref[u]
            for core in range(2):
                row = ((slab // 2) * 4 + core * 2 + slab % 2) * 80
                rows = pl.ds(pl.multiple_of(row, 16), 80)
                for i in range(4):
                    if u < 7:
                        block = units[u][i, core * 80 : core * 80 + 80, :]
                    else:
                        block = tails[i // 2][i % 2, core * 80 : core * 80 + 80, :]
                    a_all[rows, i * 512 : i * 512 + 512] = block

    for m in range(0, 1280, 320):
        total = None
        at = 0
        for piece in pieces:
            depth = piece.shape[0]
            part = jnp.dot(
                a_all[m : m + 320, at : at + depth],
                piece[...],
                preferred_element_type=F32,
            )
            total = part if total is None else total + part
            at += depth
        out_ref[m : m + 320, :] = total.astype(BF)


def matmul(slabs, units, tails, pieces):
    width = pieces[0].shape[1]
    tile = 256
    full = lambda v: pl.BlockSpec(v.shape, lambda j, s: (0,) * v.ndim)
    cols = lambda v: pl.BlockSpec((v.shape[0], tile), lambda j, s: (0, j))
    return pl.pallas_call(
        matmul_kernel,
        grid_spec=pltpu.PrefetchScalarGridSpec(
            num_scalar_prefetch=1,
            grid=(pl.cdiv(width, tile),),
            in_specs=[full(v) for v in units + tails] + [cols(v) for v in pieces],
            out_specs=pl.BlockSpec((1280, tile), lambda j, s: (0, j)),
            scratch_shapes=[pltpu.VMEM((1280, 2048), BF)],
        ),
        out_shape=jax.ShapeDtypeStruct((1280, width), BF),
        compiler_params=pltpu.CompilerParams(vmem_limit_bytes=40 * 2**20),
        cost_estimate=pl.CostEstimate(
            flops=2 * 1280 * 2048 * width,
            bytes_accessed=2 * (1280 * 2048 + 2048 * width + 1280 * width),
            transcendentals=0,
        ),
    )(slabs, *units, *tails, *pieces)


def gather_rows(out_grad):
    x = lax.axis_index("x")
    quarters = out_grad.T.reshape(4, 160, 512)
    pick = lambda by: lax.dynamic_index_in_dim(quarters, (x + by) % 4, 0, keepdims=False)
    own = jnp.stack(
        [pick(0), shift(pick(1), "x", 1), shift(pick(3), "x", -1), shift(pick(2), "x", 2)]
    )
    before = shift(own, "y", 1)
    after = shift(own, "y", -1)
    across = shift(own, "zl", 1)
    opposite = shift(after, "y", -1)
    across_before = shift(across, "y", 1)
    across_after = shift(after, "zl", 1)
    tails = [shift(across_after[:2], "y", -1), shift(across_before[2:], "y", 1)]
    units = [own, before, after, opposite, across, across_before, across_after]
    zl, y = lax.axis_index("zl"), lax.axis_index("y")
    slabs = jnp.stack(
        [
            z * 4 + (y + by) % 4
            for z, steps in ((zl, (0, 3, 1, 2)), (1 - zl, (0, 3, 1, 2)))
            for by in steps
        ]
    ).astype(jnp.int32)
    return slabs, units, tails


def gather_tokens(hidden):
    before = shift(hidden, "x", 1)
    after = shift(hidden, "x", -1)
    return [
        hidden,
        before,
        after,
        shift(before[:256], "x", 1),
        shift(after[256:], "x", -1),
    ]


def on_device(gate_pre, up_pre, out_grad, master, moment_one, moment_two):
    x, c = lax.axis_index("x"), lax.axis_index("c")
    slabs, units, tails = gather_rows(out_grad)
    grads = []
    for start, width in CHUNKS:
        gate = gate_pre[:, start : start + width].astype(F32)
        up = up_pre[:, start : start + width].astype(F32)
        hidden = (jax.nn.silu(gate) * up).astype(BF)
        partial = matmul(slabs, units, tails, gather_tokens(hidden))
        summed = lax.psum_scatter(partial, ("zh", "c"), scatter_dimension=0, tiled=True)
        summed = summed.reshape(2, 80, width)
        first = lax.dynamic_index_in_dim(summed, c, 0, keepdims=False)
        second = lax.dynamic_index_in_dim(summed, 1 - c, 0, keepdims=False)
        devices = [(i, j) for i in range(4) for j in range(2)]
        first = lax.ppermute(
            first, ("x", "c"), [(2 * i + j, 2 * (2 * j + i // 2) + i % 2) for i, j in devices]
        )
        second = lax.ppermute(
            second,
            ("x", "c"),
            [(2 * i + j, 2 * (2 * (1 - j) + i // 2) + i % 2) for i, j in devices],
        )
        low = x < 2
        grads.append(
            jnp.concatenate([jnp.where(low, first, second), jnp.where(low, second, first)], axis=0)
        )
    grad = jnp.concatenate(grads, axis=1).astype(F32)
    moment_one_new = 0.9 * moment_one + 0.1 * grad
    moment_two_new = 0.95 * moment_two + 0.05 * grad * grad
    first = moment_one_new / (1.0 - 0.9**20)
    second = moment_two_new / (1.0 - 0.95**20)
    master_new = master - 0.01 * (first / (jnp.sqrt(second) + 1e-08) + 0.1 * master)
    serving = lax.all_to_all(
        master_new.astype(BF), ("zl", "y"), split_axis=0, concat_axis=1, tiled=True
    )
    return (master_new, moment_one_new, moment_two_new, serving)


def solution(mesh):
    fine = Mesh(mesh.devices.reshape(4, 4, 2, 2, 4), ("zh", "x", "c", "zl", "y"))
    placed = P(("zh", "x", "c"), ("zl", "y"))
    return jax.shard_map(
        on_device,
        mesh=fine,
        in_specs=(placed,) * 6,
        out_specs=(placed, placed, placed, P(("zh", "x", "c", "zl", "y"), None)),
        check_vma=False,
    )
```

time: 311 us -> 220 us (0.71)
  waiting for transfers between devices: 238 us -> 114 us
  starting transfers between devices: 0.08 us -> 36.5 us
  Pallas kernels: 0 us -> 18.1 us
  matrix products: 15.9 us -> 0 us
  local copies, waits for them, and re-layouts: 23.6 us -> 13 us
  other arithmetic: 3.61 us -> 7.58 us
    reduce_scatter x1 -> x2, waiting for transfers between devices: 168 us -> 45.9 us  [on_device(): lax.psum_scatter(partial, ('zh', 'c'), scatter_dimension=0, tiled=True)]
    all_gather x1 -> x0, waiting for transfers between devices: 69.9 us -> none  [on_device(): full_grad = lax.all_gather(out_grad, 'tensor', axis=1, tiled=True)]
    ppermute x0 -> x23, waiting for transfers between devices: none -> 67.9 us  [the longest x19 61.2 us: shift(): return lax.ppermute(value, axis, [(i, (i + by) % n) for i in range(n)])]
    ppermute x0 -> x23, starting transfers between devices: none -> 36.4 us  [the longest x19 30.4 us: shift(): return lax.ppermute(value, axis, [(i, (i + by) % n) for i in range(n)])]
    pallas_call x0 -> x2, Pallas kernels: none -> 18.1 us  [matmul(): pl.pallas_call(matmul_kernel, grid_spec=pltpu.PrefetchScalarGridSpec(num_...]
    unnamed x7 -> x30, local copies, waits for them, and re-layouts: 23.4 us -> 6.17 us
    dot_general x1 -> x0, matrix products: 15.9 us -> none  [on_device(): lax.dot_general(full_grad, hidden, contract, preferred_element_type=jnp.f...]
    convert_element_type x1 -> x3, other arithmetic: 3.61 us -> 7.44 us  [the longest x2 3.99 us: on_device(): hidden = (jax.nn.silu(gate) * up).astype(BF)]
  transfers between devices with their start and end apart: 2 -> 25, of which waited for: 2 -> 17; matrix products, arithmetic and copies ran while one was open for 0% -> 4% of each run, Pallas kernels for 0% -> 5%
where the time goes in v1:
time: 220 us
  waiting for transfers between devices  114 us (52%)
  starting transfers between devices  36.5 us (17%)
  Pallas kernels  18.1 us (8%)
  blocking collectives  16.6 us (8%)
  between operations  14.3 us (6%)
  local copies, waits for them, and re-layouts  13 us (6%)
  other arithmetic  7.58 us (3%)
    ppermute x19, waiting for transfers between devices, shift(): return lax.ppermute(value, axis, [(i, (i + by) % n) for i in range(n)])  61.2 us
    reduce_scatter x2, waiting for transfers between devices, on_device(): lax.psum_scatter(partial, ('zh', 'c'), scatter_dimension=0, tiled=True)  45.9 us
    ppermute x19, starting transfers between devices, shift(): return lax.ppermute(value, axis, [(i, (i + by) % n) for i in range(n)])  30.4 us
    pallas_call x2, Pallas kernels, matmul(): pl.pallas_call(matmul_kernel, grid_spec=pltpu.PrefetchScalarGridSpec(num_...  18.1 us
    all_to_all x1, blocking collectives, on_device(): lax.all_to_all(master_new.astype(BF), ('zl', 'y'), split_axis=0, concat_a...  16.6 us
    ppermute x2, waiting for transfers between devices, on_device(): lax.ppermute(first, ('x', 'c'), [(2 * i + j, 2 * (2 * j + i // 2) + i % 2...  6.52 us
    unnamed x30, local copies, waits for them, and re-layouts  6.17 us
    ppermute x2, starting transfers between devices, on_device(): lax.ppermute(first, ('x', 'c'), [(2 * i + j, 2 * (2 * j + i // 2) + i % 2...  4.78 us
  transfers between devices with their start and end apart: 25, of which 17 were waited for; matrix products, arithmetic and copies ran while one was open for 4% of the time, Pallas kernels for 5%

profile of v1, /device:TPU:4, one launch (start us, length us, event | category | flops | bytes accessed | tf_op | source)
XLA Modules:
  0.0 219.9 jit_solution(7067638450748543501)
XLA Ops:
  7.3 1.3 copy.13
  8.6 0.1 constant_dynamic-slice_fusion
  8.7 1.3 collective-permute-start
  10.0 0.8 collective-permute-start.1
  10.8 3.5 %collective-permute-start.2 = (bf16[160,512]{1,0:T(8,128)(2,1)S(1)}, bf16[160,512]{1,0:T(8,128)(2,1)S(1)}, u32[]{:S(2)}, u32[]{:S(2)}) collective-permute-start(bf16[160,512]{1,0:T(8,128)(2,1)S(1)} %get-tuple-element.9), channel_id=1, source_target_pairs={{0,32},{16,48},{32,0},{48,16},{1,33},{17,49},{33,1},{49,17},{2,34}... | collective-permute-start | bytes 491528 | tf_op jit(solution)/shard_map/ppermute | solution.py:17
  14.2 0.9 collective-permute-done
  15.2 2.1 collective-permute-done.1
  17.3 0.9 collective-permute-done.2
  18.2 0.1 pad_maximum_fusion.refs_0_
  18.3 2.0 collective-permute-start.6
  20.3 3.0 %collective-permute-start.4 = (bf16[4,160,512]{2,1,0:T(8,128)(2,1)S(1)}, bf16[4,160,512]{2,1,0:T(8,128)(2,1)}, u32[]{:S(2)}, u32[]{:S(2)}) collective-permute-start(bf16[4,160,512]{2,1,0:T(8,128)(2,1)S(1)} %pad_maximum_fusion.refs_0_), channel_id=1, source_target_pairs={{0,3},{1,0},{2,1},{3,2},{4,7},{5,4},{6,5},{7,6},{8,11},{9,8},{10,9... | collective-permute-start | bytes 1966088 | tf_op jit(solution)/shard_map/ppermute | solution.py:17
  23.3 1.9 fusion.9.refs_9_
  25.2 2.7 %collective-permute-start.17 = (bf16[512,768]{1,0:T(8,128)(2,1)S(1)}, bf16[512,768]{1,0:T(8,128)(2,1)S(1)}, u32[]{:S(2)}, u32[]{:S(2)}) collective-permute-start(bf16[512,768]{1,0:T(8,128)(2,1)S(1)} %fusion.9.refs_9_), channel_id=1, source_target_pairs={{0,16},{16,32},{32,48},{48,0},{1,17},{17,33},{33,49},{49,1},{2,18}... | collective-permute-start | bytes 2359304 | tf_op jit(solution)/shard_map/ppermute | solution.py:17
  27.9 6.2 %collective-permute-done.6.refs_4_ = bf16[4,160,512]{2,1,0:T(8,128)(2,1)S(1)} collective-permute-done((bf16[4,160,512]{2,1,0:T(8,128)(2,1)S(1)}, bf16[4,160,512]{2,1,0:T(8,128)(2,1)S(1)}, u32[]{:S(2)}, u32[]{:S(2)}) %collective-permute-start.6) | collective-permute-done | bytes 655392 | tf_op jit(solution)/shard_map/ppermute | solution.py:17
  34.0 1.6 collective-permute-start.7
  35.6 0.4 collective-permute-done.4.refs_2_
  36.0 1.3 collective-permute-start.8
  37.4 1.6 collective-permute-start.3
  38.9 4.5 %collective-permute-done.17.refs_10_ = bf16[512,768]{1,0:T(8,128)(2,1)S(1)} collective-permute-done((bf16[512,768]{1,0:T(8,128)(2,1)S(1)}, bf16[512,768]{1,0:T(8,128)(2,1)S(1)}, u32[]{:S(2)}, u32[]{:S(2)}) %collective-permute-start.17) | collective-permute-done | bytes 786464 | tf_op jit(solution)/shard_map/ppermute | solution.py:17
  43.4 0.7 collective-permute-start.5
  44.2 0.8 slice.44
  45.0 3.0 %collective-permute-start.19 = (bf16[256,768]{1,0:T(8,128)(2,1)}, bf16[256,768]{1,0:T(8,128)(2,1)S(1)}, u32[]{:S(2)}, u32[]{:S(2)}) collective-permute-start(bf16[256,768]{1,0:T(8,128)(2,1)} %slice.44), channel_id=1, source_target_pairs={{0,16},{16,32},{32,48},{48,0},{1,17},{17,33},{33,49},{49,1},{2,18}... | collective-permute-start | bytes 1179656 | tf_op jit(solution)/shard_map/ppermute | solution.py:17
  47.9 0.8 slice.45
  48.7 4.2 %collective-permute-done.7.refs_5_ = bf16[4,160,512]{2,1,0:T(8,128)(2,1)S(1)} collective-permute-done((bf16[4,160,512]{2,1,0:T(8,128)(2,1)S(1)}, bf16[4,160,512]{2,1,0:T(8,128)(2,1)S(1)}, u32[]{:S(2)}, u32[]{:S(2)}) %collective-permute-start.7) | collective-permute-done | bytes 655392 | tf_op jit(solution)/shard_map/ppermute | solution.py:17
  52.9 2.2 collective-permute-start.20
  55.1 0.7 slice.41
  55.9 0.4 collective-permute-start.10
  56.3 0.7 slice.40
  57.0 9.9 %collective-permute-done.3.refs_1_ = bf16[4,160,512]{2,1,0:T(8,128)(2,1)S(1)} collective-permute-done((bf16[4,160,512]{2,1,0:T(8,128)(2,1)S(1)}, bf16[4,160,512]{2,1,0:T(8,128)(2,1)S(1)}, u32[]{:S(2)}, u32[]{:S(2)}) %collective-permute-start.3) | collective-permute-done | bytes 655392 | tf_op jit(solution)/shard_map/ppermute | solution.py:17
  67.0 0.8 copy-done.9
  67.8 1.8 collective-permute-start.9
  69.6 0.1 stack.48.slab_ref
  69.7 1.6 collective-permute-done.10.refs_8_
  71.3 3.9 %collective-permute-done.9.refs_7_ = bf16[2,160,512]{2,1,0:T(8,128)(2,1)} collective-permute-done((bf16[2,160,512]{2,1,0:T(8,128)(2,1)}, bf16[2,160,512]{2,1,0:T(8,128)(2,1)}, u32[]{:S(2)}, u32[]{:S(2)}) %collective-permute-start.9) | collective-permute-done | bytes 327712 | tf_op jit(solution)/shard_map/ppermute | solution.py:17
  75.2 1.1 copy-done.1
  76.3 1.1 copy-done.4
  77.4 1.1 copy-done.7
  78.5 1.1 copy-done.10
  79.5 8.1 %shard_map.94 = bf16[1280,768]{1,0:T(8,128)(2,1)} custom-call(s32[8]{0:T(128)S(1)} %stack.48.slab_ref, bf16[4,160,512]{2,1,0:T(8,128)(2,1)S(1)} %pad_maximum_fusion.refs_0_, bf16[4,160,512]{2,1,0:T(8,128)(2,1)S(1)} %copy-done.10, bf16[4,160,512]{2,1,0:T(8,128)(2,1)} %collective-permute-done.4.refs_2_, bf16[4,160,512]{2,1,0:T(8,128)(2,1)} %collective-permute-done.5.refs_3_, ...), custom_call_target="tpu_custom_call" | custom-call | flops 4026531840 | bytes 10354688 | tf_op jit(solution)/shard_map/pallas_call | solution.py:58
  87.7 0.0 reduce-scatter.3.cloned.1.call-start
  87.8 2.1 fusion.4.refs_9_
  89.9 2.2 %collective-permute-start.11 = (bf16[512,896]{1,0:T(8,128)(2,1)S(1)}, bf16[512,896]{1,0:T(8,128)(2,1)S(1)}, u32[]{:S(2)}, u32[]{:S(2)}) collective-permute-start(bf16[512,896]{1,0:T(8,128)(2,1)S(1)} %fusion.4.refs_9_), channel_id=1, source_target_pairs={{0,16},{16,32},{32,48},{48,0},{1,17},{17,33},{33,49},{49,1},{2,18}... | collective-permute-start | bytes 2752520 | tf_op jit(solution)/shard_map/ppermute | solution.py:17
  92.1 0.1 collective-permute-start.12
  92.3 18.3 %collective-permute-done.11.refs_10_ = bf16[512,896]{1,0:T(8,128)(2,1)S(1)} collective-permute-done((bf16[512,896]{1,0:T(8,128)(2,1)S(1)}, bf16[512,896]{1,0:T(8,128)(2,1)S(1)}, u32[]{:S(2)}, u32[]{:S(2)}) %collective-permute-start.11) | collective-permute-done | bytes 917536 | tf_op jit(solution)/shard_map/ppermute | solution.py:17
  110.6 0.4 collective-permute-start.13
  111.1 1.8 collective-permute-start.14
  112.8 6.3 %collective-permute-done.13.refs_12_ = bf16[256,896]{1,0:T(8,128)(2,1)S(1)} collective-permute-done((bf16[256,896]{1,0:T(8,128)(2,1)S(1)}, bf16[256,896]{1,0:T(8,128)(2,1)S(1)}, u32[]{:S(2)}, u32[]{:S(2)}) %collective-permute-start.13) | collective-permute-done | bytes 458784 | tf_op jit(solution)/shard_map/ppermute | solution.py:17
  119.2 1.9 collective-permute-done.14.refs_13_
  121.1 9.9 %shard_map.93 = bf16[1280,896]{1,0:T(8,128)(2,1)} custom-call(s32[8]{0:T(128)S(1)} %stack.48.slab_ref, bf16[4,160,512]{2,1,0:T(8,128)(2,1)S(1)} %pad_maximum_fusion.refs_0_, bf16[4,160,512]{2,1,0:T(8,128)(2,1)S(1)} %copy-done.11, bf16[4,160,512]{2,1,0:T(8,128)(2,1)} %collective-permute-done.4.refs_2_, bf16[4,160,512]{2,1,0:T(8,128)(2,1)} %collective-permute-done.5.refs_3_, ...), custom_call_target="tpu_custom_call" | custom-call | flops 4697620480 | bytes 11206656 | tf_op jit(solution)/shard_map/pallas_call | solution.py:58
  131.1 3.0 %reduce-scatter.5.cloned.1.call-done = bf16[160,768]{1,0:T(8,128)(2,1)} async-done(((bf16[1280,768]{1,0:T(8,128)(2,1)}), bf16[160,768]{1,0:T(8,128)(2,1)}) %reduce-scatter.5.cloned.1.call-update) | async-done | bytes 245776 | tf_op jit(solution)/shard_map/reduce_scatter | solution.py:124
  134.1 1.1 dynamic-slice_bitcast_fusion.6
  135.2 2.4 %collective-permute-start.21 = (bf16[80,768]{1,0:T(8,128)(2,1)S(1)}, bf16[80,768]{1,0:T(8,128)(2,1)S(1)}, u32[]{:S(2)}, u32[]{:S(2)}) collective-permute-start(bf16[80,768]{1,0:T(8,128)(2,1)S(1)} %get-tuple-element.18), channel_id=1, source_target_pairs={{0,0},{8,32},{16,8},{24,40},{32,16},{40,48},{48,24},{56,56},{1,1},... | collective-permute-start | bytes 368648 | tf_op jit(solution)/shard_map/ppermute | solution.py:129
  137.7 0.7 collective-permute-start.22
  138.4 42.9 %reduce-scatter.3.cloned.1.call-done = bf16[160,896]{1,0:T(8,128)(2,1)} async-done(((bf16[1280,896]{1,0:T(8,128)(2,1)}), bf16[160,896]{1,0:T(8,128)(2,1)}) %reduce-scatter.3.cloned.1.call-update) | async-done | bytes 286736 | tf_op jit(solution)/shard_map/reduce_scatter | solution.py:124
  181.2 1.0 dynamic-slice_bitcast_fusion.4
  182.2 2.4 %collective-permute-start.15 = (bf16[80,896]{1,0:T(8,128)(2,1)S(1)}, bf16[80,896]{1,0:T(8,128)(2,1)S(1)}, u32[]{:S(2)}, u32[]{:S(2)}) collective-permute-start(bf16[80,896]{1,0:T(8,128)(2,1)S(1)} %get-tuple-element.14), channel_id=1, source_target_pairs={{0,0},{8,32},{16,8},{24,40},{32,16},{40,48},{48,24},{56,56},{1,1},... | collective-permute-start | bytes 430088 | tf_op jit(solution)/shard_map/ppermute | solution.py:129
  184.6 0.5 collective-permute-start.16
  185.2 6.5 %collective-permute-done.15 = bf16[80,896]{1,0:T(8,128)(2,1)S(1)} collective-permute-done((bf16[80,896]{1,0:T(8,128)(2,1)S(1)}, bf16[80,896]{1,0:T(8,128)(2,1)S(1)}, u32[]{:S(2)}, u32[]{:S(2)}) %collective-permute-start.15) | collective-permute-done | bytes 143392 | tf_op jit(solution)/shard_map/ppermute | solution.py:129
  191.7 0.1 collective-permute-done.16
  191.9 3.4 %fusion.12 = (bf16[160,1664]{1,0:T(8,128)(2,1)S(1)}, f32[160,1664]{1,0:T(8,128)}, f32[160,1664]{1,0:T(8,128)}, f32[160,1664]{1,0:T(8,128)}) fusion(f32[160,1664]{1,0:T(8,128)S(1)} %copy-done.12, bf16[80,768]{1,0:T(8,128)(2,1)S(1)} %get-tuple-element.17, bf16[80,768]{1,0:T(8,128)(2,1)S(1)} %get-tuple-element.16, bf16[80,896]{1,0:T(8,128)(2,1)S(1)} %get-tuple-element.13, ...), kind=kLoop, calls=%fused_computation.33 | loop fusion | flops 6389760 | bytes 7454720 | tf_op jit(solution)/shard_map/convert_element_type | solution.py:148
  195.3 0.1 all_to_all.14
  195.4 16.6 %all_to_all.19 = bf16[8,20,1664]{2,1,0:T(8,128)(2,1)S(1)} all-to-all(bf16[8,20,1664]{2,1,0:T(8,128)(2,1)S(1)} %all_to_all.14), channel_id=1, replica_groups=mesh['zh'=4,'x'=4,'c'=2,'zl'=2,'y'=4] {'zl','y'}, dimensions={0} | all-to-all | bytes 1064960 | tf_op jit(solution)/shard_map/all_to_all | solution.py:147
  212.0 0.1 copy.14
  212.1 0.9 copy.15
  (40 shorter events, 0.3 us)
Async XLA Ops:
  7.2 126.9 %reduce-scatter.5.cloned.1.call-start = ((), (), s32[]{:S(2)}) async-start(), calls=%async_computation.4 | async-start | bytes 2211840 | tf_op jit(solution)/shard_map/reduce_scatter | solution.py:124
  8.7 6.5 %collective-permute-start = (bf16[160,512]{1,0:T(8,128)(2,1)S(1)}, bf16[160,512]{1,0:T(8,128)(2,1)S(1)}, u32[]{:S(2)}, u32[]{:S(2)}) collective-permute-start(bf16[160,512]{1,0:T(8,128)(2,1)S(1)} %get-tuple-element.11), channel_id=1, source_target_pairs={{0,16},{16,32},{32,48},{48,0},{1,17},{17,33},{33,49},{49,1},{2,18}... | collective-permute-start | bytes 491528 | tf_op jit(solution)/shard_map/ppermute | solution.py:17
  10.0 7.3 %collective-permute-start.1 = (bf16[160,512]{1,0:T(8,128)(2,1)S(1)}, bf16[160,512]{1,0:T(8,128)(2,1)S(1)}, u32[]{:S(2)}, u32[]{:S(2)}) collective-permute-start(bf16[160,512]{1,0:T(8,128)(2,1)S(1)} %get-tuple-element.10), channel_id=1, source_target_pairs={{0,48},{16,0},{32,16},{48,32},{1,49},{17,1},{33,17},{49,33},{2,50}... | collective-permute-start | bytes 491528 | tf_op jit(solution)/shard_map/ppermute | solution.py:17
  10.8 7.4 %collective-permute-start.2 = (bf16[160,512]{1,0:T(8,128)(2,1)S(1)}, bf16[160,512]{1,0:T(8,128)(2,1)S(1)}, u32[]{:S(2)}, u32[]{:S(2)}) collective-permute-start(bf16[160,512]{1,0:T(8,128)(2,1)S(1)} %get-tuple-element.9), channel_id=1, source_target_pairs={{0,32},{16,48},{32,0},{48,16},{1,33},{17,49},{33,1},{49,17},{2,34}... | collective-permute-start | bytes 491528 | tf_op jit(solution)/shard_map/ppermute | solution.py:17
  18.3 15.7 %collective-permute-start.6 = (bf16[4,160,512]{2,1,0:T(8,128)(2,1)S(1)}, bf16[4,160,512]{2,1,0:T(8,128)(2,1)S(1)}, u32[]{:S(2)}, u32[]{:S(2)}) collective-permute-start(bf16[4,160,512]{2,1,0:T(8,128)(2,1)S(1)} %pad_maximum_fusion.refs_0_), channel_id=1, source_target_pairs={{0,4},{4,0},{1,5},{5,1},{2,6},{6,2},{3,7},{7,3},{8,12},{12,8},{9,1... | collective-permute-start | bytes 1966088 | tf_op jit(solution)/shard_map/ppermute | solution.py:17
  20.3 15.7 %collective-permute-start.4 = (bf16[4,160,512]{2,1,0:T(8,128)(2,1)S(1)}, bf16[4,160,512]{2,1,0:T(8,128)(2,1)}, u32[]{:S(2)}, u32[]{:S(2)}) collective-permute-start(bf16[4,160,512]{2,1,0:T(8,128)(2,1)S(1)} %pad_maximum_fusion.refs_0_), channel_id=1, source_target_pairs={{0,3},{1,0},{2,1},{3,2},{4,7},{5,4},{6,5},{7,6},{8,11},{9,8},{10,9... | collective-permute-start | bytes 1966088 | tf_op jit(solution)/shard_map/ppermute | solution.py:17
  25.2 18.2 %collective-permute-start.17 = (bf16[512,768]{1,0:T(8,128)(2,1)S(1)}, bf16[512,768]{1,0:T(8,128)(2,1)S(1)}, u32[]{:S(2)}, u32[]{:S(2)}) collective-permute-start(bf16[512,768]{1,0:T(8,128)(2,1)S(1)} %fusion.9.refs_9_), channel_id=1, source_target_pairs={{0,16},{16,32},{32,48},{48,0},{1,17},{17,33},{33,49},{49,1},{2,18}... | collective-permute-start | bytes 2359304 | tf_op jit(solution)/shard_map/ppermute | solution.py:17
  27.9 17.1 %collective-permute-start.18 = (bf16[512,768]{1,0:T(8,128)(2,1)S(1)}, bf16[512,768]{1,0:T(8,128)(2,1)S(1)}, u32[]{:S(2)}, u32[]{:S(2)}) collective-permute-start(bf16[512,768]{1,0:T(8,128)(2,1)S(1)} %fusion.9.refs_9_), channel_id=1, source_target_pairs={{0,48},{16,0},{32,16},{48,32},{1,49},{17,1},{33,17},{49,33},{2,50}... | collective-permute-start | bytes 2359304 | tf_op jit(solution)/shard_map/ppermute | solution.py:17
  34.0 21.8 %copy-start.6 = (bf16[4,160,512]{2,1,0:T(8,128)(2,1)}, bf16[4,160,512]{2,1,0:T(8,128)(2,1)S(1)}, u32[]{:S(2)}) copy-start(bf16[4,160,512]{2,1,0:T(8,128)(2,1)S(1)} %collective-permute-done.6.refs_4_) | copy-start | bytes 1966084
  34.0 18.9 %collective-permute-start.7 = (bf16[4,160,512]{2,1,0:T(8,128)(2,1)S(1)}, bf16[4,160,512]{2,1,0:T(8,128)(2,1)S(1)}, u32[]{:S(2)}, u32[]{:S(2)}) collective-permute-start(bf16[4,160,512]{2,1,0:T(8,128)(2,1)S(1)} %collective-permute-done.6.refs_4_), channel_id=1, source_target_pairs={{0,1},{1,2},{2,3},{3,0},{4,5},{5,6},{6,7},{7,4},{8,9},{9,10},{10,1... | collective-permute-start | bytes 1966088 | tf_op jit(solution)/shard_map/ppermute | solution.py:17
  36.0 19.8 %collective-permute-start.8 = (bf16[4,160,512]{2,1,0:T(8,128)(2,1)}, bf16[4,160,512]{2,1,0:T(8,128)(2,1)S(1)}, u32[]{:S(2)}, u32[]{:S(2)}) collective-permute-start(bf16[4,160,512]{2,1,0:T(8,128)(2,1)} %collective-permute-done.4.refs_2_), channel_id=1, source_target_pairs={{0,4},{4,0},{1,5},{5,1},{2,6},{6,2},{3,7},{7,3},{8,12},{12,8},{9,1... | collective-permute-start | bytes 1966088 | tf_op jit(solution)/shard_map/ppermute | solution.py:17
  37.4 29.6 %collective-permute-start.3 = (bf16[4,160,512]{2,1,0:T(8,128)(2,1)S(1)}, bf16[4,160,512]{2,1,0:T(8,128)(2,1)S(1)}, u32[]{:S(2)}, u32[]{:S(2)}) collective-permute-start(bf16[4,160,512]{2,1,0:T(8,128)(2,1)S(1)} %pad_maximum_fusion.refs_0_), channel_id=1, source_target_pairs={{0,1},{1,2},{2,3},{3,0},{4,5},{5,6},{6,7},{7,4},{8,9},{9,10},{10,1... | collective-permute-start | bytes 1966088 | tf_op jit(solution)/shard_map/ppermute | solution.py:17
  43.4 26.3 %collective-permute-start.5 = (bf16[4,160,512]{2,1,0:T(8,128)(2,1)}, bf16[4,160,512]{2,1,0:T(8,128)(2,1)}, u32[]{:S(2)}, u32[]{:S(2)}) collective-permute-start(bf16[4,160,512]{2,1,0:T(8,128)(2,1)} %collective-permute-done.4.refs_2_), channel_id=1, source_target_pairs={{0,3},{1,0},{2,1},{3,2},{4,7},{5,4},{6,5},{7,6},{8,11},{9,8},{10,9... | collective-permute-start | bytes 1966088 | tf_op jit(solution)/shard_map/ppermute | solution.py:17
  45.0 24.7 %collective-permute-start.19 = (bf16[256,768]{1,0:T(8,128)(2,1)}, bf16[256,768]{1,0:T(8,128)(2,1)S(1)}, u32[]{:S(2)}, u32[]{:S(2)}) collective-permute-start(bf16[256,768]{1,0:T(8,128)(2,1)} %slice.44), channel_id=1, source_target_pairs={{0,16},{16,32},{32,48},{48,0},{1,17},{17,33},{33,49},{49,1},{2,18}... | collective-permute-start | bytes 1179656 | tf_op jit(solution)/shard_map/ppermute | solution.py:17
  52.9 14.0 %copy-start = (bf16[4,160,512]{2,1,0:T(8,128)(2,1)}, bf16[4,160,512]{2,1,0:T(8,128)(2,1)S(1)}, u32[]{:S(2)}) copy-start(bf16[4,160,512]{2,1,0:T(8,128)(2,1)S(1)} %collective-permute-done.7.refs_5_) | copy-start | bytes 1966084
  52.9 16.8 %collective-permute-start.20 = (bf16[256,768]{1,0:T(8,128)(2,1)}, bf16[256,768]{1,0:T(8,128)(2,1)}, u32[]{:S(2)}, u32[]{:S(2)}) collective-permute-start(bf16[256,768]{1,0:T(8,128)(2,1)} %slice.45), channel_id=1, source_target_pairs={{0,48},{16,0},{32,16},{48,32},{1,49},{17,1},{33,17},{49,33},{2,50}... | collective-permute-start | bytes 1179656 | tf_op jit(solution)/shard_map/ppermute | solution.py:17
  55.9 11.1 %copy-start.3 = (bf16[4,160,512]{2,1,0:T(8,128)(2,1)}, bf16[4,160,512]{2,1,0:T(8,128)(2,1)S(1)}, u32[]{:S(2)}) copy-start(bf16[4,160,512]{2,1,0:T(8,128)(2,1)S(1)} %collective-permute-done.8.refs_6_) | copy-start | bytes 1966084
  55.9 15.5 %collective-permute-start.10 = (bf16[2,160,512]{2,1,0:T(8,128)(2,1)}, bf16[2,160,512]{2,1,0:T(8,128)(2,1)}, u32[]{:S(2)}, u32[]{:S(2)}) collective-permute-start(bf16[2,160,512]{2,1,0:T(8,128)(2,1)} %slice.41), channel_id=1, source_target_pairs={{0,1},{1,2},{2,3},{3,0},{4,5},{5,6},{6,7},{7,4},{8,9},{9,10},{10,1... | collective-permute-start | bytes 983048 | tf_op jit(solution)/shard_map/ppermute | solution.py:17
  67.0 0.8 copy-start.9
  67.8 7.4 %collective-permute-start.9 = (bf16[2,160,512]{2,1,0:T(8,128)(2,1)}, bf16[2,160,512]{2,1,0:T(8,128)(2,1)}, u32[]{:S(2)}, u32[]{:S(2)}) collective-permute-start(bf16[2,160,512]{2,1,0:T(8,128)(2,1)} %slice.40), channel_id=1, source_target_pairs={{0,3},{1,0},{2,1},{3,2},{4,7},{5,4},{6,5},{7,6},{8,11},{9,8},{10,9... | collective-permute-start | bytes 983048 | tf_op jit(solution)/shard_map/ppermute | solution.py:17
  75.2 1.1 copy-start.1
  76.3 1.1 copy-start.4
  77.4 1.1 copy-start.7
  78.5 1.1 copy-start.10
  87.7 93.5 %reduce-scatter.3.cloned.1.call-start = ((), (), s32[]{:S(2)}) async-start(), calls=%async_computation.3 | async-start | bytes 2580480 | tf_op jit(solution)/shard_map/reduce_scatter | solution.py:124
  87.8 33.3 %copy-start.8 = (bf16[4,160,512]{2,1,0:T(8,128)(2,1)S(1)}, bf16[4,160,512]{2,1,0:T(8,128)(2,1)}, u32[]{:S(2)}) copy-start(bf16[4,160,512]{2,1,0:T(8,128)(2,1)} %copy-done.6) | copy-start | bytes 1966084
  87.8 33.3 %copy-start.11 = (bf16[4,160,512]{2,1,0:T(8,128)(2,1)S(1)}, bf16[4,160,512]{2,1,0:T(8,128)(2,1)}, u32[]{:S(2)}) copy-start(bf16[4,160,512]{2,1,0:T(8,128)(2,1)} %copy-done.9) | copy-start | bytes 1966084
  89.9 31.2 %copy-start.2 = (bf16[4,160,512]{2,1,0:T(8,128)(2,1)S(1)}, bf16[4,160,512]{2,1,0:T(8,128)(2,1)}, u32[]{:S(2)}) copy-start(bf16[4,160,512]{2,1,0:T(8,128)(2,1)} %copy-done) | copy-start | bytes 1966084
  89.9 31.2 %copy-start.5 = (bf16[4,160,512]{2,1,0:T(8,128)(2,1)S(1)}, bf16[4,160,512]{2,1,0:T(8,128)(2,1)}, u32[]{:S(2)}) copy-start(bf16[4,160,512]{2,1,0:T(8,128)(2,1)} %copy-done.3) | copy-start | bytes 1966084
  89.9 20.6 %collective-permute-start.11 = (bf16[512,896]{1,0:T(8,128)(2,1)S(1)}, bf16[512,896]{1,0:T(8,128)(2,1)S(1)}, u32[]{:S(2)}, u32[]{:S(2)}) collective-permute-start(bf16[512,896]{1,0:T(8,128)(2,1)S(1)} %fusion.4.refs_9_), channel_id=1, source_target_pairs={{0,16},{16,32},{32,48},{48,0},{1,17},{17,33},{33,49},{49,1},{2,18}... | collective-permute-start | bytes 2752520 | tf_op jit(solution)/shard_map/ppermute | solution.py:17
  92.1 18.9 %collective-permute-start.12 = (bf16[512,896]{1,0:T(8,128)(2,1)S(1)}, bf16[512,896]{1,0:T(8,128)(2,1)S(1)}, u32[]{:S(2)}, u32[]{:S(2)}) collective-permute-start(bf16[512,896]{1,0:T(8,128)(2,1)S(1)} %fusion.4.refs_9_), channel_id=1, source_target_pairs={{0,48},{16,0},{32,16},{48,32},{1,49},{17,1},{33,17},{49,33},{2,50}... | collective-permute-start | bytes 2752520 | tf_op jit(solution)/shard_map/ppermute | solution.py:17
  110.6 8.6 %collective-permute-start.13 = (bf16[256,896]{1,0:T(8,128)(2,1)S(1)}, bf16[256,896]{1,0:T(8,128)(2,1)S(1)}, u32[]{:S(2)}, u32[]{:S(2)}) collective-permute-start(bf16[256,896]{1,0:T(8,128)(2,1)S(1)} %slice.42), channel_id=1, source_target_pairs={{0,16},{16,32},{32,48},{48,0},{1,17},{17,33},{33,49},{49,1},{2,18}... | collective-permute-start | bytes 1376264 | tf_op jit(solution)/shard_map/ppermute | solution.py:17
  111.1 10.0 %collective-permute-start.14 = (bf16[256,896]{1,0:T(8,128)(2,1)S(1)}, bf16[256,896]{1,0:T(8,128)(2,1)S(1)}, u32[]{:S(2)}, u32[]{:S(2)}) collective-permute-start(bf16[256,896]{1,0:T(8,128)(2,1)S(1)} %slice.43), channel_id=1, source_target_pairs={{0,48},{16,0},{32,16},{48,32},{1,49},{17,1},{33,17},{49,33},{2,50}... | collective-permute-start | bytes 1376264 | tf_op jit(solution)/shard_map/ppermute | solution.py:17
  134.1 57.7 %copy-start.12 = (f32[160,1664]{1,0:T(8,128)S(1)}, f32[160,1664]{1,0:T(8,128)}, u32[]{:S(2)}) copy-start(f32[160,1664]{1,0:T(8,128)} %param.9) | copy-start | bytes 3194884
  134.1 57.7 %copy-start.13 = (f32[160,1664]{1,0:T(8,128)S(1)}, f32[160,1664]{1,0:T(8,128)}, u32[]{:S(2)}) copy-start(f32[160,1664]{1,0:T(8,128)} %param.10) | copy-start | bytes 3194884
  135.2 49.9 %collective-permute-start.21 = (bf16[80,768]{1,0:T(8,128)(2,1)S(1)}, bf16[80,768]{1,0:T(8,128)(2,1)S(1)}, u32[]{:S(2)}, u32[]{:S(2)}) collective-permute-start(bf16[80,768]{1,0:T(8,128)(2,1)S(1)} %get-tuple-element.18), channel_id=1, source_target_pairs={{0,0},{8,32},{16,8},{24,40},{32,16},{40,48},{48,24},{56,56},{1,1},... | collective-permute-start | bytes 368648 | tf_op jit(solution)/shard_map/ppermute | solution.py:129
  137.7 47.5 %collective-permute-start.22 = (bf16[80,768]{1,0:T(8,128)(2,1)S(1)}, bf16[80,768]{1,0:T(8,128)(2,1)S(1)}, u32[]{:S(2)}, u32[]{:S(2)}) collective-permute-start(bf16[80,768]{1,0:T(8,128)(2,1)S(1)} %get-tuple-element.19), channel_id=1, source_target_pairs={{0,32},{8,0},{16,40},{24,8},{32,48},{40,16},{48,56},{56,24},{1,33}... | collective-permute-start | bytes 368648 | tf_op jit(solution)/shard_map/ppermute | solution.py:132
  182.2 9.4 %collective-permute-start.15 = (bf16[80,896]{1,0:T(8,128)(2,1)S(1)}, bf16[80,896]{1,0:T(8,128)(2,1)S(1)}, u32[]{:S(2)}, u32[]{:S(2)}) collective-permute-start(bf16[80,896]{1,0:T(8,128)(2,1)S(1)} %get-tuple-element.14), channel_id=1, source_target_pairs={{0,0},{8,32},{16,8},{24,40},{32,16},{40,48},{48,24},{56,56},{1,1},... | collective-permute-start | bytes 430088 | tf_op jit(solution)/shard_map/ppermute | solution.py:129
  184.6 7.2 %collective-permute-start.16 = (bf16[80,896]{1,0:T(8,128)(2,1)S(1)}, bf16[80,896]{1,0:T(8,128)(2,1)S(1)}, u32[]{:S(2)}, u32[]{:S(2)}) collective-permute-start(bf16[80,896]{1,0:T(8,128)(2,1)S(1)} %get-tuple-element.15), channel_id=1, source_target_pairs={{0,32},{8,0},{16,40},{24,8},{32,48},{40,16},{48,56},{56,24},{1,33}... | collective-permute-start | bytes 430088 | tf_op jit(solution)/shard_map/ppermute | solution.py:132
Sparse Core Ops, SparseCore 0:
  87.8 46.2 reduce-scatter.4
  136.8 44.3 reduce-scatter.2
